TPU v7x, 256 devices: a whole 4x4x8 slice. The times are simulated.
256 devices in a mesh: coarse: 16 (over x_hi, y, core), fine: 16 (over x_lo, z).
Axes of the slice: x: 4 (x_hi: 2, x_lo: 2; x = x_hi * 2 + x_lo), y: 4, z: 8, core: 2. Of those that a mesh axis runs over, the one named last changes fastest.
Arguments:
- activations: bfloat16 [131072, 1280], P(('coarse', 'fine')), may hold values from -6 to 6
- targets: int32 [131072], P(('coarse', 'fine')), may hold values from 0 to 4
- inner_squeeze_weight: bfloat16 [1280, 640], replicated, may hold values from -0.15625 to 0.15625
- inner_filter_taps: bfloat16 [3, 640, 640], replicated, may hold values from -0.125 to 0.125
- inner_expand_weight: bfloat16 [640, 1280], replicated, may hold values from -0.25 to 0.25
- outer_squeeze_weight: bfloat16 [1280, 640], replicated, may hold values from -0.15625 to 0.15625
- outer_filter_taps: bfloat16 [3, 640, 640], replicated, may hold values from -0.125 to 0.125
- outer_expand_weight: bfloat16 [640, 1280], replicated, may hold values from -0.25 to 0.25
- decoder: bfloat16 [5, 1280], replicated, may hold values from -0.059814453 to 0.059814453
Outputs:
- input_gradient: bfloat16 [131072, 1280], P(('coarse', 'fine'))
- token_loss: float32 [131072], P(('coarse', 'fine'))
All inputs are finite; a program needn't handle non-finite values.
Results may differ from a plain program's by a relative error of at most 0.015.
Values may be sent and summed in bfloat16 or wider, within the bound.
A program may use at most 64 MiB of HBM per device.

v0:
```python
import math

import jax
import jax.numpy as jnp
from jax import lax
from jax.sharding import PartitionSpec as P

COARSE_HOP = 4


eps = 1e-05


def from_behind(value, axis, steps):
    count = lax.axis_size(axis)
    pairs = [(source, (source + steps) % count) for source in range(count)]
    return lax.ppermute(value, axis, pairs)


def norm_rows(values):
    average = jnp.mean(values, axis=-1, keepdims=True)
    centred = values - average
    factor = lax.rsqrt(jnp.mean(centred * centred, axis=-1, keepdims=True) + eps)
    return (centred * factor, factor)


def norm_back(normal, factor, upward):
    first_term = upward - jnp.mean(upward, axis=-1, keepdims=True)
    return (first_term - normal * jnp.mean(upward * normal, axis=-1, keepdims=True)) * factor


def gelu_exact(inputs):
    return 0.5 * inputs * (1.0 + lax.erf(inputs * (1.0 / math.sqrt(2.0))))


def gelu_slope(inputs):
    return 0.5 * (1.0 + lax.erf(inputs * (1.0 / math.sqrt(2.0)))) + inputs * jnp.exp(
        -0.5 * inputs * inputs
    ) * (1.0 / math.sqrt(2.0 * math.pi))


def product(leading, trailing):
    return jnp.dot(leading, trailing, preferred_element_type=jnp.float32)


def product_t(leading, trailing):
    return lax.dot_general(
        leading, trailing, (((1,), (1,)), ((), ())), preferred_element_type=jnp.float32
    )


def inner_pair(shard_rows):
    behind_rows = from_behind(shard_rows, ("coarse", "fine"), 2)
    ahead_rows = from_behind(shard_rows, ("coarse", "fine"), -2)
    return (behind_rows, ahead_rows)


def outer_pair(shard_rows):
    behind_rows = from_behind(shard_rows, "coarse", COARSE_HOP)
    ahead_rows = from_behind(shard_rows, "coarse", -COARSE_HOP)
    return (behind_rows, ahead_rows)


def residual_block_forward(block_in, squeeze, taps, expand, neighbours):
    normal_in, _ = norm_rows(block_in.astype(jnp.float32))
    entry_act = gelu_exact(normal_in).astype(jnp.bfloat16)
    squeezed = product(entry_act, squeeze)
    normal_mid, _ = norm_rows(squeezed)
    middle = gelu_exact(normal_mid).astype(jnp.bfloat16)
    behind_rows, ahead_rows = neighbours(middle)
    conv_sum = (
        product(behind_rows, taps[0]) + product(middle, taps[1]) + product(ahead_rows, taps[2])
    )
    normal_conv, _ = norm_rows(conv_sum)
    closing = gelu_exact(normal_conv).astype(jnp.bfloat16)
    block_out = (block_in.astype(jnp.float32) + product(closing, expand)).astype(jnp.bfloat16)
    return (block_out, squeezed, conv_sum)


def residual_block_backward(
    block_in, squeezed, conv_sum, squeeze, taps, expand, neighbours, gradient_result
):
    dclosing = product_t(gradient_result.astype(jnp.bfloat16), expand)
    normal_conv, factor_conv = norm_rows(conv_sum)
    dconv = norm_back(normal_conv, factor_conv, gelu_slope(normal_conv) * dclosing).astype(
        jnp.bfloat16
    )
    behind_rows, ahead_rows = neighbours(dconv)
    dmiddle = (
        product_t(ahead_rows, taps[0]) + product_t(dconv, taps[1]) + product_t(behind_rows, taps[2])
    )
    normal_mid, factor_mid = norm_rows(squeezed)
    dsqueezed = norm_back(normal_mid, factor_mid, gelu_slope(normal_mid) * dmiddle).astype(
        jnp.bfloat16
    )
    dentry = product_t(dsqueezed, squeeze)
    normal_in, factor_in = norm_rows(block_in.astype(jnp.float32))
    return gradient_result + norm_back(normal_in, factor_in, gelu_slope(normal_in) * dentry)


def on_device(
    activations,
    targets,
    inner_squeeze_weight,
    inner_filter_taps,
    inner_expand_weight,
    outer_squeeze_weight,
    outer_filter_taps,
    outer_expand_weight,
    decoder,
):
    outer_block_input, inner_bottleneck_rows, inner_convolved = residual_block_forward(
        activations, inner_squeeze_weight, inner_filter_taps, inner_expand_weight, inner_pair
    )
    final_output, outer_bottleneck_rows, outer_convolved = residual_block_forward(
        outer_block_input, outer_squeeze_weight, outer_filter_taps, outer_expand_weight, outer_pair
    )
    normal_final, factor_final = norm_rows(final_output.astype(jnp.float32))
    normed = normal_final.astype(jnp.bfloat16)
    logits = product_t(normed, decoder)
    exponent = jnp.exp(logits)
    totals = jnp.sum(exponent, axis=-1, keepdims=True)
    classes = jnp.arange(decoder.shape[0], dtype=jnp.int32)
    onehot = (targets[:, None] == classes[None, :]).astype(jnp.float32)
    token_loss = jnp.log(totals[:, 0]) - jnp.sum(logits * onehot, axis=-1)
    dlogits = (32.0 * (exponent / totals - onehot)).astype(jnp.bfloat16)
    gradient_result = norm_back(normal_final, factor_final, product(dlogits, decoder))
    gradient_result = residual_block_backward(
        outer_block_input,
        outer_bottleneck_rows,
        outer_convolved,
        outer_squeeze_weight,
        outer_filter_taps,
        outer_expand_weight,
        outer_pair,
        gradient_result,
    )
    gradient_result = residual_block_backward(
        activations,
        inner_bottleneck_rows,
        inner_convolved,
        inner_squeeze_weight,
        inner_filter_taps,
        inner_expand_weight,
        inner_pair,
        gradient_result,
    )
    return (gradient_result.astype(jnp.bfloat16), token_loss)


def solution(mesh):
    in_specs = (
        P(("coarse", "fine"), None),
        P(("coarse", "fine")),
        P(),
        P(),
        P(),
        P(),
        P(),
        P(),
        P(),
    )
    out_specs = (P(("coarse", "fine"), None), P(("coarse", "fine")))
    return jax.shard_map(
        on_device, mesh=mesh, in_specs=in_specs, out_specs=out_specs, check_vma=False
    )
```

profile of v0, /device:TPU:41, one launch (start us, length us, event | category | flops | bytes accessed | tf_op | source)
XLA Modules:
  0.0 176.3 jit_solution(10350064386199572912)
XLA Ops:
  0.7 1.7 convert_reduce_fusion.1
  3.0 3.2 %fusion.153 = (f32[512]{0:T(512)S(1)}, f32[512,640]{1,0:T(8,128)S(1)}) fusion(bf16[1280,640]{1,0:T(8,128)(2,1)} %param.11, bf16[512,1280]{1,0:T(8,128)(2,1)S(1)} %copy-done.1, f32[512]{0:T(512)S(1)} %add_rsqrt_fusion.6, f32[512]{0:T(512)S(1)} %broadcast_multiply_fusion.20), kind=kOutput, calls=%fused_computation.226 | convolution fusion | flops 844430848 | bytes 4265984 | tf_op jit(solution)/shard_map/dot_general | solution.py:43
  6.9 6.7 %collective-permute-start.1 = (bf16[512,640]{1,0:T(8,128)(2,1)S(1)}, bf16[512,640]{1,0:T(8,128)(2,1)S(1)}, u32[]{:S(2)}, u32[]{:S(2)}) collective-permute-start(bf16[512,640]{1,0:T(8,128)(2,1)S(1)} %multiply_convert_fusion.7), channel_id=1, source_target_pairs={{0,254},{1,255},{2,0},{3,1},{4,2},{5,3},{6,4},{7,5},{8,6},{9,7},{1... | collective-permute-start | bytes 1966088 | tf_op jit(solution)/shard_map/ppermute | solution.py:17
  14.3 25.6 %collective-permute-done.1 = bf16[512,640]{1,0:T(8,128)(2,1)S(1)} collective-permute-done((bf16[512,640]{1,0:T(8,128)(2,1)S(1)}, bf16[512,640]{1,0:T(8,128)(2,1)S(1)}, u32[]{:S(2)}, u32[]{:S(2)}) %collective-permute-start.1) | collective-permute-done | bytes 655392 | tf_op jit(solution)/shard_map/ppermute | solution.py:17
  40.7 7.2 %collective-permute-done = bf16[512,640]{1,0:T(8,128)(2,1)S(1)} collective-permute-done((bf16[512,640]{1,0:T(8,128)(2,1)S(1)}, bf16[512,640]{1,0:T(8,128)(2,1)S(1)}, u32[]{:S(2)}, u32[]{:S(2)}) %collective-permute-start) | collective-permute-done | bytes 655392 | tf_op jit(solution)/shard_map/ppermute | solution.py:17
  47.8 0.9 fusion.154
  49.2 1.5 convert_reduce_fusion
  51.2 1.7 fusion.155
  53.7 2.2 %collective-permute-start.3 = (bf16[512,640]{1,0:T(8,128)(2,1)S(1)}, bf16[512,640]{1,0:T(8,128)(2,1)S(1)}, u32[]{:S(2)}, u32[]{:S(2)}) collective-permute-start(bf16[512,640]{1,0:T(8,128)(2,1)S(1)} %multiply_convert_fusion.5), channel_id=1, source_target_pairs={{0,192},{16,208},{32,224},{48,240},{64,0},{80,16},{96,32},{112,48}... | collective-permute-start | bytes 1966088 | tf_op jit(solution)/shard_map/ppermute | solution.py:17
  55.9 0.9 collective-permute-start.2
  57.5 27.7 %collective-permute-done.3 = bf16[512,640]{1,0:T(8,128)(2,1)S(1)} collective-permute-done((bf16[512,640]{1,0:T(8,128)(2,1)S(1)}, bf16[512,640]{1,0:T(8,128)(2,1)S(1)}, u32[]{:S(2)}, u32[]{:S(2)}) %collective-permute-start.3) | collective-permute-done | bytes 655392 | tf_op jit(solution)/shard_map/ppermute | solution.py:17
  86.0 0.9 fusion.156
  87.2 1.5 convert_reduce_fusion.2
  90.1 1.0 fusion.148
  91.1 2.1 %fusion.152 = (f32[512]{0:T(512)S(1)}, f32[512]{0:T(512)S(1)}, f32[512,640]{1,0:T(8,128)S(1)}) fusion(f32[512]{0:T(512)S(1)} %add_rsqrt_fusion.1, f32[512,640]{1,0:T(8,128)S(1)} %get-tuple-element.27, f32[512]{0:T(512)S(1)} %broadcast_multiply_fusion.8, bf16[640,1280]{1,0:T(8,128)(2,1)S(1)} %copy-done, f32[512]{0:T(512)S(1)} %get-tuple-element.38, ...), kind=kOutput, calls=%fused_computation.225 | convolution fusion | flops 848690176 | bytes 8208384 | tf_op jit(solution)/shard_map/dot_general | solution.py:47
  93.7 2.0 %collective-permute-start.5 = (bf16[512,640]{1,0:T(8,128)(2,1)S(1)}, bf16[512,640]{1,0:T(8,128)(2,1)S(1)}, u32[]{:S(2)}, u32[]{:S(2)}) collective-permute-start(bf16[512,640]{1,0:T(8,128)(2,1)S(1)} %multiply_convert_fusion.3), channel_id=1, source_target_pairs={{0,64},{16,80},{32,96},{48,112},{64,128},{80,144},{96,160},{112,17... | collective-permute-start | bytes 1966088 | tf_op jit(solution)/shard_map/ppermute | solution.py:17
  95.6 3.5 %collective-permute-start.4 = (bf16[512,640]{1,0:T(8,128)(2,1)S(1)}, bf16[512,640]{1,0:T(8,128)(2,1)S(1)}, u32[]{:S(2)}, u32[]{:S(2)}) collective-permute-start(bf16[512,640]{1,0:T(8,128)(2,1)S(1)} %multiply_convert_fusion.3), channel_id=1, source_target_pairs={{0,192},{16,208},{32,224},{48,240},{64,0},{80,16},{96,32},{112,48}... | collective-permute-start | bytes 1966088 | tf_op jit(solution)/shard_map/ppermute | solution.py:17
  99.1 0.8 fusion.92
  99.9 22.2 %collective-permute-done.5 = bf16[512,640]{1,0:T(8,128)(2,1)S(1)} collective-permute-done((bf16[512,640]{1,0:T(8,128)(2,1)S(1)}, bf16[512,640]{1,0:T(8,128)(2,1)S(1)}, u32[]{:S(2)}, u32[]{:S(2)}) %collective-permute-start.5) | collective-permute-done | bytes 655392 | tf_op jit(solution)/shard_map/ppermute | solution.py:17
  122.1 0.8 fusion.88
  122.9 5.0 %collective-permute-done.4 = bf16[512,640]{1,0:T(8,128)(2,1)S(1)} collective-permute-done((bf16[512,640]{1,0:T(8,128)(2,1)S(1)}, bf16[512,640]{1,0:T(8,128)(2,1)S(1)}, u32[]{:S(2)}, u32[]{:S(2)}) %collective-permute-start.4) | collective-permute-done | bytes 655392 | tf_op jit(solution)/shard_map/ppermute | solution.py:17
  127.9 1.5 fusion.151
  129.4 2.4 %fusion.147 = (f32[512]{0:T(512)S(1)}, f32[512]{0:T(512)S(1)}, f32[512,1280]{1,0:T(8,128)S(1)}) fusion(f32[512]{0:T(512)S(1)} %add_rsqrt_fusion.3, f32[512]{0:T(512)S(1)} %broadcast_multiply_fusion.19, bf16[512,1280]{1,0:T(8,128)(2,1)S(1)} %get-tuple-element.23, bf16[1280,640]{1,0:T(8,128)(2,1)S(1)} %copy-done.6, f32[512,640]{1,0:T(8,128)S(1)} %get-tuple-element.33, ...), kind=kOutput, calls=%fused_computation.220 | convolution fusion | flops 850983936 | bytes 8208384 | tf_op jit(solution)/shard_map/dot_general | solution.py:47
  131.8 1.7 fusion.27
  133.5 1.7 fusion.150
  135.7 4.7 %collective-permute-start.6 = (bf16[512,640]{1,0:T(8,128)(2,1)S(1)}, bf16[512,640]{1,0:T(8,128)(2,1)S(1)}, u32[]{:S(2)}, u32[]{:S(2)}) collective-permute-start(bf16[512,640]{1,0:T(8,128)(2,1)S(1)} %multiply_convert_fusion.1), channel_id=1, source_target_pairs={{0,254},{1,255},{2,0},{3,1},{4,2},{5,3},{6,4},{7,5},{8,6},{9,7},{1... | collective-permute-start | bytes 1966088 | tf_op jit(solution)/shard_map/ppermute | solution.py:17
  141.0 0.8 fusion.102
  141.8 27.8 %collective-permute-done.7 = bf16[512,640]{1,0:T(8,128)(2,1)S(1)} collective-permute-done((bf16[512,640]{1,0:T(8,128)(2,1)S(1)}, bf16[512,640]{1,0:T(8,128)(2,1)S(1)}, u32[]{:S(2)}, u32[]{:S(2)}) %collective-permute-start.7) | collective-permute-done | bytes 655392 | tf_op jit(solution)/shard_map/ppermute | solution.py:17
  169.7 0.8 fusion.98
  170.5 1.4 fusion.149
  172.0 2.4 %fusion.146 = (f32[512]{0:T(512)S(1)}, f32[512]{0:T(512)S(1)}, f32[512,1280]{1,0:T(8,128)S(1)}) fusion(f32[512]{0:T(512)S(1)} %add_rsqrt_fusion.6, f32[512]{0:T(512)S(1)} %broadcast_multiply_fusion.20, bf16[512,1280]{1,0:T(8,128)(2,1)S(1)} %copy-done.1, bf16[1280,640]{1,0:T(8,128)(2,1)S(1)} %copy-done.8, f32[512,640]{1,0:T(8,128)S(1)} %get-tuple-element.36, ...), kind=kOutput, calls=%fused_computation.219 | convolution fusion | flops 850983936 | bytes 8208384 | tf_op jit(solution)/shard_map/dot_general | solution.py:47
  174.4 1.9 %fusion.39 = bf16[512,1280]{1,0:T(8,128)(2,1)} fusion(f32[512,1280]{1,0:T(8,128)S(1)} %fusion.27, bf16[512,1280]{1,0:T(8,128)(2,1)S(1)} %copy-done.1, f32[512,1280]{1,0:T(8,128)S(1)} %get-tuple-element.37, f32[512]{0:T(512)S(1)} %broadcast_multiply_fusion.12, f32[512]{0:T(512)S(1)} %broadcast_multiply_fusion.13, f32[512]{0:T(512)S(1)} %add_rsqrt_fusion.6, ...), kind=kLoop, calls=%fused_computation.51 | loop fusion | flops 5898240 | bytes 7872512 | tf_op jit(solution)/shard_map/convert_element_type | solution.py:148
  (66 shorter events, 9.3 us)
Async XLA Ops:
  0.6 86.6 %copy-start = (bf16[640,1280]{1,0:T(8,128)(2,1)S(1)}, bf16[640,1280]{1,0:T(8,128)(2,1)}, u32[]{:S(2)}) copy-start(bf16[640,1280]{1,0:T(8,128)(2,1)} %param.16) | copy-start | bytes 4915204
  0.6 1.8 %copy-start.1 = (bf16[512,1280]{1,0:T(8,128)(2,1)S(1)}, bf16[512,1280]{1,0:T(8,128)(2,1)}, u32[]{:S(2)}) copy-start(bf16[512,1280]{1,0:T(8,128)(2,1)} %param.9) | copy-start | bytes 3932164
  6.1 7.4 %copy-start.3 = (bf16[3,640,640]{2,1,0:T(8,128)(2,1)S(1)}, bf16[3,640,640]{2,1,0:T(8,128)(2,1)}, u32[]{:S(2)}) copy-start(bf16[3,640,640]{2,1,0:T(8,128)(2,1)} %param.12) | copy-start | bytes 7372804
  6.9 33.0 %collective-permute-start.1 = (bf16[512,640]{1,0:T(8,128)(2,1)S(1)}, bf16[512,640]{1,0:T(8,128)(2,1)S(1)}, u32[]{:S(2)}, u32[]{:S(2)}) collective-permute-start(bf16[512,640]{1,0:T(8,128)(2,1)S(1)} %multiply_convert_fusion.7), channel_id=1, source_target_pairs={{0,254},{1,255},{2,0},{3,1},{4,2},{5,3},{6,4},{7,5},{8,6},{9,7},{1... | collective-permute-start | bytes 1966088 | tf_op jit(solution)/shard_map/ppermute | solution.py:17
  13.5 34.3 %collective-permute-start = (bf16[512,640]{1,0:T(8,128)(2,1)S(1)}, bf16[512,640]{1,0:T(8,128)(2,1)S(1)}, u32[]{:S(2)}, u32[]{:S(2)}) collective-permute-start(bf16[512,640]{1,0:T(8,128)(2,1)S(1)} %multiply_convert_fusion.7), channel_id=1, source_target_pairs={{0,2},{1,3},{2,4},{3,5},{4,6},{5,7},{6,8},{7,9},{8,10},{9,11},{10,... | collective-permute-start | bytes 1966088 | tf_op jit(solution)/shard_map/ppermute | solution.py:17
  47.8 1.4 copy-start.7
  49.2 2.0 %copy-start.6 = (bf16[1280,640]{1,0:T(8,128)(2,1)S(1)}, bf16[1280,640]{1,0:T(8,128)(2,1)}, u32[]{:S(2)}) copy-start(bf16[1280,640]{1,0:T(8,128)(2,1)} %param.14) | copy-start | bytes 4915204
  53.0 3.8 %copy-start.2 = (bf16[3,640,640]{2,1,0:T(8,128)(2,1)S(1)}, bf16[3,640,640]{2,1,0:T(8,128)(2,1)}, u32[]{:S(2)}) copy-start(bf16[3,640,640]{2,1,0:T(8,128)(2,1)} %param.15) | copy-start | bytes 7372804
  53.7 31.5 %collective-permute-start.3 = (bf16[512,640]{1,0:T(8,128)(2,1)S(1)}, bf16[512,640]{1,0:T(8,128)(2,1)S(1)}, u32[]{:S(2)}, u32[]{:S(2)}) collective-permute-start(bf16[512,640]{1,0:T(8,128)(2,1)S(1)} %multiply_convert_fusion.5), channel_id=1, source_target_pairs={{0,192},{16,208},{32,224},{48,240},{64,0},{80,16},{96,32},{112,48}... | collective-permute-start | bytes 1966088 | tf_op jit(solution)/shard_map/ppermute | solution.py:17
  55.9 30.1 %collective-permute-start.2 = (bf16[512,640]{1,0:T(8,128)(2,1)S(1)}, bf16[512,640]{1,0:T(8,128)(2,1)S(1)}, u32[]{:S(2)}, u32[]{:S(2)}) collective-permute-start(bf16[512,640]{1,0:T(8,128)(2,1)S(1)} %multiply_convert_fusion.5), channel_id=1, source_target_pairs={{0,64},{16,80},{32,96},{48,112},{64,128},{80,144},{96,160},{112,17... | collective-permute-start | bytes 1966088 | tf_op jit(solution)/shard_map/ppermute | solution.py:17
  88.7 0.7 copy-start.4
  88.7 0.7 copy-start.5
  93.7 28.5 %collective-permute-start.5 = (bf16[512,640]{1,0:T(8,128)(2,1)S(1)}, bf16[512,640]{1,0:T(8,128)(2,1)S(1)}, u32[]{:S(2)}, u32[]{:S(2)}) collective-permute-start(bf16[512,640]{1,0:T(8,128)(2,1)S(1)} %multiply_convert_fusion.3), channel_id=1, source_target_pairs={{0,64},{16,80},{32,96},{48,112},{64,128},{80,144},{96,160},{112,17... | collective-permute-start | bytes 1966088 | tf_op jit(solution)/shard_map/ppermute | solution.py:17
  95.6 32.3 %collective-permute-start.4 = (bf16[512,640]{1,0:T(8,128)(2,1)S(1)}, bf16[512,640]{1,0:T(8,128)(2,1)S(1)}, u32[]{:S(2)}, u32[]{:S(2)}) collective-permute-start(bf16[512,640]{1,0:T(8,128)(2,1)S(1)} %multiply_convert_fusion.3), channel_id=1, source_target_pairs={{0,192},{16,208},{32,224},{48,240},{64,0},{80,16},{96,32},{112,48}... | collective-permute-start | bytes 1966088 | tf_op jit(solution)/shard_map/ppermute | solution.py:17
  135.6 34.1 %collective-permute-start.7 = (bf16[512,640]{1,0:T(8,128)(2,1)S(1)}, bf16[512,640]{1,0:T(8,128)(2,1)S(1)}, u32[]{:S(2)}, u32[]{:S(2)}) collective-permute-start(bf16[512,640]{1,0:T(8,128)(2,1)S(1)} %multiply_convert_fusion.1), channel_id=1, source_target_pairs={{0,2},{1,3},{2,4},{3,5},{4,6},{5,7},{6,8},{7,9},{8,10},{9,11},{10,... | collective-permute-start | bytes 1966088 | tf_op jit(solution)/shard_map/ppermute | solution.py:17
  135.7 34.8 %collective-permute-start.6 = (bf16[512,640]{1,0:T(8,128)(2,1)S(1)}, bf16[512,640]{1,0:T(8,128)(2,1)S(1)}, u32[]{:S(2)}, u32[]{:S(2)}) collective-permute-start(bf16[512,640]{1,0:T(8,128)(2,1)S(1)} %multiply_convert_fusion.1), channel_id=1, source_target_pairs={{0,254},{1,255},{2,0},{3,1},{4,2},{5,3},{6,4},{7,5},{8,6},{9,7},{1... | collective-permute-start | bytes 1966088 | tf_op jit(solution)/shard_map/ppermute | solution.py:17
  170.5 1.5 copy-start.8
where the time goes:
time: 177 us; the launch traced here: 176 us
  waiting for transfers between devices  116 us (66%)
  matrix products  29 us (16%)
  starting transfers between devices  20 us (11%)
  other arithmetic  10.2 us (6%)
    ppermute x8, waiting for transfers between devices, from_behind(): return lax.ppermute(value, axis, pairs)  116 us
    ppermute x8, starting transfers between devices, from_behind(): return lax.ppermute(value, axis, pairs)  20 us
    dot_general x11, matrix products, product_t(): lax.dot_general(leading, trailing, (((1,), (1,)), ((), ())), preferred_el...  15.4 us
    dot_general x11, matrix products, product(): return jnp.dot(leading, trailing, preferred_element_type=jnp.float32)  13.6 us
  transfers between devices with their start and end apart: 8, of which 6 were waited for; matrix products, arithmetic and copies ran while one was open for 4% of the time, Pallas kernels for 0%

commit v1 on v0

v1 whole, which is shorter than its diff:
```python
import functools
import math

import jax
import jax.numpy as jnp
from jax import lax
from jax.experimental import pallas as pl
from jax.experimental.pallas import tpu as pltpu
from jax.sharding import PartitionSpec as P

MESH = pl.DeviceIdType.MESH
F32, BF16 = jnp.float32, jnp.bfloat16
EPS = 1e-05
ROWS, D, BOT, VOCAB = 512, 1280, 640, 5
CHUNKS = 4
CH = ROWS // CHUNKS
QUARTER = CH // 4
EXTRA = 128
WIDE = D + EXTRA
TILE = 16


def normed(values):
    centred = values - jnp.mean(values, axis=-1, keepdims=True)
    factor = lax.rsqrt(jnp.mean(centred * centred, axis=-1, keepdims=True) + EPS)
    return centred * factor, factor


def norm_back(normal, factor, upward):
    first = upward - jnp.mean(upward, axis=-1, keepdims=True)
    return (first - normal * jnp.mean(upward * normal, axis=-1, keepdims=True)) * factor


def gelu(s):
    return 0.5 * s * (1.0 + lax.erf(s * (1.0 / math.sqrt(2.0))))


def slope(s):
    return 0.5 * (1.0 + lax.erf(s * (1.0 / math.sqrt(2.0)))) + s * jnp.exp(-0.5 * s * s) * (
        1.0 / math.sqrt(2.0 * math.pi)
    )


def dot(a, b):
    return jnp.dot(a, b, preferred_element_type=F32)


def dot_t(a, b):
    return lax.dot_general(a, b, (((1,), (1,)), ((), ())), preferred_element_type=F32)


def tiles(body, unroll=4):
    def step(i, carry):
        body(pl.multiple_of(i * TILE, TILE))
        return carry

    lax.fori_loop(0, CH // TILE, step, 0, unroll=unroll)


def lanes(column):
    return jnp.broadcast_to(column, (column.shape[0], 128))


def kernel(
    x_hbm, targets, dec, sq_i_hbm, taps_i_hbm, ex_i_hbm, sq_o_hbm, taps_o_hbm, ex_o_hbm,
    out_hbm, loss_out,
    x, sq_i, taps_i, ex_i, sq_o, taps_o, ex_o,
    n_in, f_in, n_mid, f_mid, n_conv, f_conv, sl_in, sl_mid,
    mid, mid_behind, mid_ahead, dconv, dconv_behind, dconv_ahead,
    xo_send, xo, g_send, g,
    ent, wide, narrow, outs,
    o_n_in, o_f_in, o_n_mid, o_f_mid, o_n_conv, o_f_conv, o_grad, o_mid, o_dconv,
    w_sem, x_sem, own_sem, out_sem, halo_send, halo_recv, turn_send, turn_recv,
):
    c, f = lax.axis_index("coarse"), lax.axis_index("fine")
    shard = c * 16 + f
    mine = c // 4

    def inner_partner(way):
        other = lax.rem(shard + (2 if way == 0 else 254), 256)
        return (other // 16, lax.rem(other, 16))

    def outer_partner(i):
        return (lax.rem(c + 4 * i, 16), f)

    barrier = pltpu.get_barrier_semaphore()
    for partner in (inner_partner(0), inner_partner(1), outer_partner(1), outer_partner(2), outer_partner(3)):
        pl.semaphore_signal(barrier, inc=1, device_id=partner, device_id_type=MESH)

    def x_copy(k):
        rows = pl.ds(pl.multiple_of(k * CH, CH), CH)
        return pltpu.make_async_copy(x_hbm.at[rows], x.at[rows], x_sem.at[k])

    weights = [
        pltpu.make_async_copy(src, dst, w_sem.at[i])
        for i, (src, dst) in enumerate(
            (
                (sq_i_hbm, sq_i), (taps_i_hbm, taps_i), (ex_i_hbm, ex_i),
                (sq_o_hbm, sq_o), (taps_o_hbm, taps_o), (ex_o_hbm, ex_o),
            )
        )
    ]
    x_copy(0).start()
    weights[0].start()
    for k in range(1, CHUNKS):
        x_copy(k).start()
    for weight in weights[1:]:
        weight.start()

    def halo(stage, way, k, source, target):
        rows = pl.ds(pl.multiple_of(k * CH, CH), CH)
        return pltpu.make_async_remote_copy(
            src_ref=source.at[rows],
            dst_ref=target.at[rows],
            send_sem=halo_send.at[stage, way, k],
            recv_sem=halo_recv.at[stage, way, k],
            device_id=inner_partner(way),
            device_id_type=MESH,
        )

    def mid_halos(k):
        return halo(0, 0, k, mid, mid_behind), halo(0, 1, k, mid, mid_ahead)

    def dconv_halos(k):
        return halo(1, 0, k, dconv, dconv_behind), halo(1, 1, k, dconv, dconv_ahead)

    def quarter(k, which):
        return pl.ds(pl.multiple_of(k * CH + which * QUARTER, QUARTER), QUARTER)

    def turn(stage, i, k, source, target):
        theirs = lax.rem(mine + i, 4)
        return pltpu.make_async_remote_copy(
            src_ref=source.at[quarter(k, theirs)],
            dst_ref=target.at[quarter(k, mine)],
            send_sem=turn_send.at[stage, i, k],
            recv_sem=turn_recv.at[stage, i, k],
            device_id=outer_partner(i),
            device_id_type=MESH,
        )

    def turns(stage, k):
        source, target = ((xo_send, xo), (g_send, g))[stage]
        return [turn(stage, i, k, source, target) for i in (1, 2, 3)] + [
            pltpu.make_async_copy(source.at[quarter(k, mine)], target.at[quarter(k, mine)], own_sem.at[stage, k])
        ]

    def await_turns(stage, k):
        *remote, own = turns(stage, k)
        for copy in remote:
            copy.wait_recv()
        own.wait()

    def at(k, r, rows=TILE):
        return pl.ds(pl.multiple_of(k * CH + r, TILE), rows)

    def enter(k):
        x_copy(k).wait()

        def first(r):
            n, factor = normed(x[at(k, r), :].astype(F32))
            n_in[at(k, r), :] = n
            f_in[at(k, r), :] = lanes(factor)
            ent[pl.ds(r, TILE), :] = gelu(n).astype(BF16)

        tiles(first)
        narrow[...] = dot(ent[...], sq_i[...])

        def second(r):
            n, factor = normed(narrow[pl.ds(r, TILE), :])
            n_mid[at(k, r), :] = n
            f_mid[at(k, r), :] = lanes(factor)
            mid[at(k, r), :] = gelu(n).astype(BF16)

        tiles(second)
        for copy in mid_halos(k):
            copy.start()

    def prepare(k):
        classes = lax.broadcasted_iota(jnp.int32, (EXTRA, CH), 0)
        columns = (classes == targets[k]).astype(F32).astype(BF16)
        eye = (classes == lax.broadcasted_iota(jnp.int32, (EXTRA, CH), 1)).astype(F32).astype(BF16)
        xo_send[at(k, 0, CH), D:] = dot_t(eye, columns).astype(BF16)

        def first(r):
            sl_in[at(k, r), :] = slope(n_in[at(k, r), :])
            sl_mid[at(k, r), :] = slope(n_mid[at(k, r), :])

        tiles(first)

    def converse(k):
        for copy in mid_halos(k):
            copy.wait_recv()
        rows = at(k, 0, CH)
        narrow[...] = (
            dot(mid_behind[rows, :], taps_i[0]) + dot(mid[rows, :], taps_i[1]) + dot(mid_ahead[rows, :], taps_i[2])
        )

        def first(r):
            n, factor = normed(narrow[pl.ds(r, TILE), :])
            n_conv[at(k, r), :] = n
            f_conv[at(k, r), :] = lanes(factor)
            ent[pl.ds(r, TILE), :BOT] = gelu(n).astype(BF16)

        tiles(first)
        wide[...] = dot(ent[:, :BOT], ex_i[...])

        def second(r):
            xo_send[at(k, r), :D] = (x[at(k, r), :].astype(F32) + wide[pl.ds(r, TILE), :]).astype(BF16)

        tiles(second)
        for copy in turns(0, k):
            copy.start()

    def around(padded):
        padded[pl.ds(0, QUARTER), :] = padded[pl.ds(CH, QUARTER), :]
        padded[pl.ds(QUARTER + CH, QUARTER), :] = padded[pl.ds(QUARTER, QUARTER), :]
        return padded[pl.ds(0, CH), :], padded[pl.ds(QUARTER, CH), :], padded[pl.ds(2 * QUARTER, CH), :]

    def outer(k):
        await_turns(0, k)

        def first(r):
            n, factor = normed(xo[at(k, r), :D].astype(F32))
            o_n_in[pl.ds(r, TILE), :] = n
            o_f_in[pl.ds(r, TILE), :] = lanes(factor)
            ent[pl.ds(r, TILE), :] = gelu(n).astype(BF16)

        tiles(first)
        narrow[...] = dot(ent[...], sq_o[...])

        def second(r):
            n, factor = normed(narrow[pl.ds(r, TILE), :])
            o_n_mid[pl.ds(r, TILE), :] = n
            o_f_mid[pl.ds(r, TILE), :] = lanes(factor)
            o_mid[pl.ds(QUARTER + r, TILE), :] = gelu(n).astype(BF16)

        tiles(second)
        behind, own, ahead = around(o_mid)
        narrow[...] = dot(behind, taps_o[0]) + dot(own, taps_o[1]) + dot(ahead, taps_o[2])

        def third(r):
            n, factor = normed(narrow[pl.ds(r, TILE), :])
            o_n_conv[pl.ds(r, TILE), :] = n
            o_f_conv[pl.ds(r, TILE), :] = lanes(factor)
            ent[pl.ds(r, TILE), :BOT] = gelu(n).astype(BF16)

        tiles(third)
        wide[...] = dot(ent[:, :BOT], ex_o[...])

        def fourth(r):
            final = (xo[at(k, r), :D].astype(F32) + wide[pl.ds(r, TILE), :]).astype(BF16)
            n, factor = normed(final.astype(F32))
            o_grad[pl.ds(r, TILE), :] = n
            narrow[pl.ds(r, TILE), :128] = lanes(factor)
            ent[pl.ds(r, TILE), :] = n.astype(BF16)

        tiles(fourth)
        logits = dot_t(ent[...], dec[...])
        lane = lax.broadcasted_iota(jnp.int32, (CH, EXTRA), 1)
        onehot = xo[at(k, 0, CH), D:].astype(F32)
        exponent = jnp.where(lane < VOCAB, jnp.exp(logits), 0.0)
        totals = jnp.sum(exponent, axis=-1, keepdims=True)
        token_loss = jnp.log(totals) - jnp.sum(logits * onehot, axis=-1, keepdims=True)
        high = token_loss.astype(BF16).astype(F32)
        g_send[at(k, 0, CH), D:] = jnp.where(
            lane == 0, high, jnp.where(lane == 1, token_loss - high, 0.0)
        ).astype(BF16)
        dlogits = (32.0 * (exponent / totals - onehot)).astype(BF16)
        wide[...] = dot(dlogits, dec[...])

        def fifth(r):
            grad = norm_back(o_grad[pl.ds(r, TILE), :], narrow[pl.ds(r, TILE), 0:1], wide[pl.ds(r, TILE), :])
            o_grad[pl.ds(r, TILE), :] = grad
            ent[pl.ds(r, TILE), :] = grad.astype(BF16)

        tiles(fifth)
        narrow[...] = dot_t(ent[...], ex_o[...])

        def sixth(r):
            n = o_n_conv[pl.ds(r, TILE), :]
            upward = slope(n) * narrow[pl.ds(r, TILE), :]
            o_dconv[pl.ds(QUARTER + r, TILE), :] = norm_back(n, o_f_conv[pl.ds(r, TILE), 0:1], upward).astype(BF16)

        tiles(sixth)
        behind, own, ahead = around(o_dconv)
        narrow[...] = dot_t(ahead, taps_o[0]) + dot_t(own, taps_o[1]) + dot_t(behind, taps_o[2])

        def seventh(r):
            n = o_n_mid[pl.ds(r, TILE), :]
            upward = slope(n) * narrow[pl.ds(r, TILE), :]
            ent[pl.ds(r, TILE), :BOT] = norm_back(n, o_f_mid[pl.ds(r, TILE), 0:1], upward).astype(BF16)

        tiles(seventh)
        wide[...] = dot_t(ent[:, :BOT], sq_o[...])

        def eighth(r):
            n = o_n_in[pl.ds(r, TILE), :]
            upward = slope(n) * wide[pl.ds(r, TILE), :]
            back = norm_back(n, o_f_in[pl.ds(r, TILE), 0:1], upward)
            g_send[at(k, r), :D] = (o_grad[pl.ds(r, TILE), :] + back).astype(BF16)

        tiles(eighth)
        for copy in turns(1, k):
            copy.start()

    def turn_back(k):
        await_turns(1, k)
        narrow[...] = dot_t(g[at(k, 0, CH), :D], ex_i[...])

        def first(r):
            n = n_conv[at(k, r), :]
            upward = slope(n) * narrow[pl.ds(r, TILE), :]
            dconv[at(k, r), :] = norm_back(n, f_conv[at(k, r), 0:1], upward).astype(BF16)

        tiles(first)
        for copy in dconv_halos(k):
            copy.start()

    def out_copy(k):
        rows = pl.ds(pl.multiple_of(k * CH, CH), CH)
        return pltpu.make_async_copy(outs.at[rows], out_hbm.at[rows], out_sem.at[k])

    def leave(k):
        loss_out[k] = dot_t(jnp.ones((8, EXTRA), BF16), g[at(k, 0, CH), D:])
        for copy in dconv_halos(k):
            copy.wait_recv()
        rows = at(k, 0, CH)
        narrow[...] = (
            dot_t(dconv_ahead[rows, :], taps_i[0])
            + dot_t(dconv[rows, :], taps_i[1])
            + dot_t(dconv_behind[rows, :], taps_i[2])
        )

        def first(r):
            upward = sl_mid[at(k, r), :] * narrow[pl.ds(r, TILE), :]
            ent[pl.ds(r, TILE), :BOT] = norm_back(n_mid[at(k, r), :], f_mid[at(k, r), 0:1], upward).astype(BF16)

        tiles(first)
        wide[...] = dot_t(ent[:, :BOT], sq_i[...])

        def second(r):
            upward = sl_in[at(k, r), :] * wide[pl.ds(r, TILE), :]
            back = norm_back(n_in[at(k, r), :], f_in[at(k, r), 0:1], upward)
            outs[at(k, r), :] = (g[at(k, r), :D].astype(F32) + back).astype(BF16)

        tiles(second)
        out_copy(k).start()

    def loop(count, body):
        def step(k, carry):
            body(k)
            return carry

        lax.fori_loop(0, count, step, 0)

    pl.semaphore_wait(barrier, 5)
    weights[0].wait()
    loop(CHUNKS, enter)
    loop(CHUNKS, prepare)
    for weight in weights[1:]:
        weight.wait()

    def middle(s):
        @pl.when(s < CHUNKS)
        def _():
            converse(s)

        @pl.when(s >= 1)
        def _():
            turn_back(s - 1)

        @pl.when(s < CHUNKS)
        def _():
            outer(s)

    loop(CHUNKS + 1, middle)
    loop(CHUNKS, leave)

    def finish(k):
        for copy in mid_halos(k) + dconv_halos(k):
            copy.wait_send()
        for stage in (0, 1):
            for copy in turns(stage, k)[:3]:
                copy.wait_send()
        out_copy(k).wait()

    loop(CHUNKS, finish)


def on_device(activations, targets, sq_i, taps_i, ex_i, sq_o, taps_o, ex_o, decoder):
    anywhere = pl.BlockSpec(memory_space=pl.ANY)
    vmem = pl.BlockSpec(memory_space=pltpu.VMEM)
    decoder = jnp.pad(decoder, ((0, EXTRA - VOCAB), (0, 0)))
    targets = targets.reshape(CHUNKS, 1, CH)
    v = pltpu.VMEM
    dma = pltpu.SemaphoreType.DMA
    out, loss = pl.pallas_call(
        kernel,
        out_shape=(
            jax.ShapeDtypeStruct((ROWS, D), BF16),
            jax.ShapeDtypeStruct((CHUNKS, 8, CH), F32),
        ),
        in_specs=[anywhere, vmem, vmem] + [anywhere] * 6,
        out_specs=(anywhere, vmem),
        scratch_shapes=[
            v((ROWS, D), BF16),
            v((D, BOT), BF16), v((3, BOT, BOT), BF16), v((BOT, D), BF16),
            v((D, BOT), BF16), v((3, BOT, BOT), BF16), v((BOT, D), BF16),
            v((ROWS, D), F32), v((ROWS, 128), F32),
            v((ROWS, BOT), F32), v((ROWS, 128), F32),
            v((ROWS, BOT), F32), v((ROWS, 128), F32),
            v((ROWS, D), F32), v((ROWS, BOT), F32),
            v((ROWS, BOT), BF16), v((ROWS, BOT), BF16), v((ROWS, BOT), BF16),
            v((ROWS, BOT), BF16), v((ROWS, BOT), BF16), v((ROWS, BOT), BF16),
            v((ROWS, WIDE), BF16), v((ROWS, WIDE), BF16), v((ROWS, WIDE), BF16), v((ROWS, WIDE), BF16),
            v((CH, D), BF16), v((CH, D), F32), v((CH, BOT), F32), v((ROWS, D), BF16),
            v((CH, D), F32), v((CH, 128), F32), v((CH, BOT), F32), v((CH, 128), F32),
            v((CH, BOT), F32), v((CH, 128), F32), v((CH, D), F32),
            v((CH + 2 * QUARTER, BOT), BF16), v((CH + 2 * QUARTER, BOT), BF16),
            dma((6,)), dma((CHUNKS,)), dma((2, CHUNKS)), dma((CHUNKS,)),
            dma((2, 2, CHUNKS)), dma((2, 2, CHUNKS)), dma((2, 4, CHUNKS)), dma((2, 4, CHUNKS)),
        ],
        compiler_params=pltpu.CompilerParams(
            collective_id=0, has_side_effects=True, vmem_limit_bytes=56 * 1024 * 1024
        ),
    )(activations, targets, decoder, sq_i, taps_i, ex_i, sq_o, taps_o, ex_o)
    return out, loss[:, 0, :].reshape(ROWS)


def solution(mesh):
    rows = P(("coarse", "fine"))
    return jax.shard_map(
        on_device,
        mesh=mesh,
        in_specs=(P(("coarse", "fine"), None), rows, P(), P(), P(), P(), P(), P(), P()),
        out_specs=(P(("coarse", "fine"), None), rows),
        check_vma=False,
    )
```

time: 177 us -> 143 us (0.81); the launches traced: 176 us -> 140 us
  Pallas kernels: 0 us -> 134 us
  waiting for transfers between devices: 116 us -> 0 us
  matrix products: 29 us -> 0 us
  starting transfers between devices: 20 us -> 0 us
  other arithmetic: 10.2 us -> 0 us
  local copies, waits for them, and re-layouts: 0.6 us -> 5.23 us
    pallas_call x0 -> x1, Pallas kernels: none -> 134 us  [on_device(): pl.pallas_call(kernel, out_shape=(jax.ShapeDtypeStruct((ROWS, D), BF16),...]
    ppermute x8 -> x0, waiting for transfers between devices: 116 us -> none  [from_behind(): return lax.ppermute(value, axis, pairs)]
    dot_general x22 -> x0, matrix products: 29 us -> none  [the longest x11 15.4 us: product_t(): lax.dot_general(leading, trailing, (((1,), (1,)), ((), ())), preferred_el...]
    ppermute x8 -> x0, starting transfers between devices: 20 us -> none  [from_behind(): return lax.ppermute(value, axis, pairs)]
    reduce_sum x8 -> x0, other arithmetic: 4.34 us -> none  [the longest x7 2.63 us: norm_rows(): jnp.mean(centred * centred, axis=-1, keepdims=True) + eps]
    convert_element_type x5 -> x0, other arithmetic: 3.45 us -> none  [the longest x1 1.9 us: on_device(): return (gradient_result.astype(jnp.bfloat16), token_loss)]
    unnamed x18 -> x1, local copies, waits for them, and re-layouts: 0.6 us -> 2.46 us
  transfers between devices with their start and end apart: 8 -> 0, of which waited for: 6 -> 0; matrix products, arithmetic and copies ran while one was open for 4% -> 0% of each run, Pallas kernels for 0% -> 0%
where the time goes in v1:
time: 143 us; the launch traced here: 140 us
  Pallas kernels  134 us (94%)
  local copies, waits for them, and re-layouts  5.23 us (4%)
    pallas_call x1, Pallas kernels, on_device(): pl.pallas_call(kernel, out_shape=(jax.ShapeDtypeStruct((ROWS, D), BF16),...  134 us

profile of v1, /device:TPU:41, one launch (start us, length us, event | category | flops | bytes accessed | tf_op | source)
XLA Modules:
  0.0 140.3 jit_solution(8896826097592628668)
XLA Ops:
  0.6 1.5 %pad.4.dec = bf16[128,1280]{1,0:T(8,128)(2,1)} pad(bf16[5,1280]{1,0:T(8,128)(2,1)} %param.17, bf16[]{:T(256)} %constant.2.clone.1), padding=0_123x0_0 | pad | bytes 340482 | tf_op jit(solution)/shard_map/jit(_pad)/pad | solution.py:393
  2.1 134.4 %shard_map.104 = (bf16[512,1280]{1,0:T(8,128)(2,1)}, f32[4,8,128]{2,1,0:T(8,128)}) custom-call(bf16[512,1280]{1,0:T(8,128)(2,1)} %x_hbm.1, s32[4,1,128]{2,1,0:T(1,128)} %bitcast.3, bf16[128,1280]{1,0:T(8,128)(2,1)} %pad.4.dec, bf16[1280,640]{1,0:T(8,128)(2,1)} %sq_i_hbm.1, bf16[3,640,640]{2,1,0:T(8,128)(2,1)} %taps_i_hbm.1, bf16[640,1280]{1,0:T(8,128)(2,1)} %ex_i_hbm.1, ...), custom_call_target="tpu_custom_call" | custom-call | tf_op jit(solution)/shard_map/pallas_call | solution.py:397
  136.5 1.3 slice.3
  137.8 2.5 %copy.12 = bf16[512,1280]{1,0:T(8,128)(2,1)} copy(bf16[512,1280]{1,0:T(8,128)(2,1)} %get-tuple-element.8) | data formatting | bytes 2621440

commit v2 on v1

--- a/solution.py
+++ b/solution.py
@@ -49,7 +49,7 @@
     return lax.dot_general(a, b, (((1,), (1,)), ((), ())), preferred_element_type=F32)
 
 
-def tiles(body, unroll=4):
+def tiles(body, unroll=CH // TILE):
     def step(i, carry):
         body(pl.multiple_of(i * TILE, TILE))
         return carry
@@ -62,15 +62,15 @@
 
 
 def kernel(
-    x_hbm, targets, dec, sq_i_hbm, taps_i_hbm, ex_i_hbm, sq_o_hbm, taps_o_hbm, ex_o_hbm,
-    out_hbm, loss_out,
+    x_hbm, targets, decoder, sq_i_hbm, taps_i_hbm, ex_i_hbm, sq_o_hbm, taps_o_hbm, ex_o_hbm,
+    outs, loss_out,
     x, sq_i, taps_i, ex_i, sq_o, taps_o, ex_o,
     n_in, f_in, n_mid, f_mid, n_conv, f_conv, sl_in, sl_mid,
     mid, mid_behind, mid_ahead, dconv, dconv_behind, dconv_ahead,
     xo_send, xo, g_send, g,
-    ent, wide, narrow, outs,
-    o_n_in, o_f_in, o_n_mid, o_f_mid, o_n_conv, o_f_conv, o_grad, o_mid, o_dconv,
-    w_sem, x_sem, own_sem, out_sem, halo_send, halo_recv, turn_send, turn_recv,
+    ent, wide, narrow,
+    o_n_in, o_f_in, o_n_mid, o_f_mid, o_n_conv, o_f_conv, o_grad, o_mid, o_dconv, dec,
+    w_sem, x_sem, own_sem, halo_send, halo_recv, turn_send, turn_recv,
 ):
     c, f = lax.axis_index("coarse"), lax.axis_index("fine")
     shard = c * 16 + f
@@ -172,8 +172,11 @@
             mid[at(k, r), :] = gelu(n).astype(BF16)
 
         tiles(second)
-        for copy in mid_halos(k):
-            copy.start()
+
+        @pl.when(k < 1)
+        def _():
+            for copy in mid_halos(k):
+                copy.start()
 
     def prepare(k):
         classes = lax.broadcasted_iota(jnp.int32, (EXTRA, CH), 0)
@@ -190,6 +193,12 @@
     def converse(k):
         for copy in mid_halos(k):
             copy.wait_recv()
+
+        @pl.when(k + 1 < CHUNKS)
+        def _():
+            for copy in mid_halos(k + 1):
+                copy.start()
+
         rows = at(k, 0, CH)
         narrow[...] = (
             dot(mid_behind[rows, :], taps_i[0]) + dot(mid[rows, :], taps_i[1]) + dot(mid_ahead[rows, :], taps_i[2])
@@ -316,12 +325,8 @@
         for copy in dconv_halos(k):
             copy.start()
 
-    def out_copy(k):
-        rows = pl.ds(pl.multiple_of(k * CH, CH), CH)
-        return pltpu.make_async_copy(outs.at[rows], out_hbm.at[rows], out_sem.at[k])
-
     def leave(k):
-        loss_out[k] = dot_t(jnp.ones((8, EXTRA), BF16), g[at(k, 0, CH), D:])
+        loss_out[k] = dot_t(jnp.ones((8, EXTRA), BF16), g[at(k, 0, CH), D:])[0:1]
         for copy in dconv_halos(k):
             copy.wait_recv()
         rows = at(k, 0, CH)
@@ -344,7 +349,6 @@
             outs[at(k, r), :] = (g[at(k, r), :D].astype(F32) + back).astype(BF16)
 
         tiles(second)
-        out_copy(k).start()
 
     def loop(count, body):
         def step(k, carry):
@@ -353,6 +357,8 @@
 
         lax.fori_loop(0, count, step, 0)
 
+    dec[...] = jnp.zeros_like(dec)
+    dec[pl.ds(0, VOCAB), :] = decoder[...]
     pl.semaphore_wait(barrier, 5)
     weights[0].wait()
     loop(CHUNKS, enter)
@@ -360,20 +366,22 @@
     for weight in weights[1:]:
         weight.wait()
 
-    def middle(s):
-        @pl.when(s < CHUNKS)
+    def middle(step):
+        s = step - 1
+
+        @pl.when(s + 1 < CHUNKS)
         def _():
-            converse(s)
+            converse(s + 1)
+
+        @pl.when(jnp.logical_and(s >= 0, s < CHUNKS))
+        def _():
+            outer(s)
 
         @pl.when(s >= 1)
         def _():
             turn_back(s - 1)
 
-        @pl.when(s < CHUNKS)
-        def _():
-            outer(s)
-
-    loop(CHUNKS + 1, middle)
+    loop(CHUNKS + 2, middle)
     loop(CHUNKS, leave)
 
     def finish(k):
@@ -382,15 +390,13 @@
         for stage in (0, 1):
             for copy in turns(stage, k)[:3]:
                 copy.wait_send()
-        out_copy(k).wait()
 
     loop(CHUNKS, finish)
 
 
 def on_device(activations, targets, sq_i, taps_i, ex_i, sq_o, taps_o, ex_o, decoder):
-    anywhere = pl.BlockSpec(memory_space=pl.ANY)
+    anywhere = pl.BlockSpec(memory_space=pltpu.HBM)
     vmem = pl.BlockSpec(memory_space=pltpu.VMEM)
-    decoder = jnp.pad(decoder, ((0, EXTRA - VOCAB), (0, 0)))
     targets = targets.reshape(CHUNKS, 1, CH)
     v = pltpu.VMEM
     dma = pltpu.SemaphoreType.DMA
@@ -398,10 +404,10 @@
         kernel,
         out_shape=(
             jax.ShapeDtypeStruct((ROWS, D), BF16),
-            jax.ShapeDtypeStruct((CHUNKS, 8, CH), F32),
+            jax.ShapeDtypeStruct((CHUNKS, 1, CH), F32),
         ),
         in_specs=[anywhere, vmem, vmem] + [anywhere] * 6,
-        out_specs=(anywhere, vmem),
+        out_specs=(vmem, vmem),
         scratch_shapes=[
             v((ROWS, D), BF16),
             v((D, BOT), BF16), v((3, BOT, BOT), BF16), v((BOT, D), BF16),
@@ -413,18 +419,18 @@
             v((ROWS, BOT), BF16), v((ROWS, BOT), BF16), v((ROWS, BOT), BF16),
             v((ROWS, BOT), BF16), v((ROWS, BOT), BF16), v((ROWS, BOT), BF16),
             v((ROWS, WIDE), BF16), v((ROWS, WIDE), BF16), v((ROWS, WIDE), BF16), v((ROWS, WIDE), BF16),
-            v((CH, D), BF16), v((CH, D), F32), v((CH, BOT), F32), v((ROWS, D), BF16),
+            v((CH, D), BF16), v((CH, D), F32), v((CH, BOT), F32),
             v((CH, D), F32), v((CH, 128), F32), v((CH, BOT), F32), v((CH, 128), F32),
             v((CH, BOT), F32), v((CH, 128), F32), v((CH, D), F32),
-            v((CH + 2 * QUARTER, BOT), BF16), v((CH + 2 * QUARTER, BOT), BF16),
-            dma((6,)), dma((CHUNKS,)), dma((2, CHUNKS)), dma((CHUNKS,)),
+            v((CH + 2 * QUARTER, BOT), BF16), v((CH + 2 * QUARTER, BOT), BF16), v((EXTRA, D), BF16),
+            dma((6,)), dma((CHUNKS,)), dma((2, CHUNKS)),
             dma((2, 2, CHUNKS)), dma((2, 2, CHUNKS)), dma((2, 4, CHUNKS)), dma((2, 4, CHUNKS)),
         ],
         compiler_params=pltpu.CompilerParams(
-            collective_id=0, has_side_effects=True, vmem_limit_bytes=56 * 1024 * 1024
+            collective_id=0, has_side_effects=True, vmem_limit_bytes=62 * 1024 * 1024
         ),
     )(activations, targets, decoder, sq_i, taps_i, ex_i, sq_o, taps_o, ex_o)
-    return out, loss[:, 0, :].reshape(ROWS)
+    return out, loss.reshape(ROWS)
 
 
 def solution(mesh):

time: 143 us -> 101 us (0.71); the launches traced: 140 us -> 101 us
  Pallas kernels: 134 us -> 97.3 us
  local copies, waits for them, and re-layouts: 5.23 us -> 3.04 us
    pallas_call x1, Pallas kernels: 134 us -> 97.3 us  [on_device(): pl.pallas_call(kernel, out_shape=(jax.ShapeDtypeStruct((ROWS, D), BF16),...]
    pad x1 -> x0, local copies, waits for them, and re-layouts: 1.48 us -> none  [on_device(): decoder = jnp.pad(decoder, ((0, EXTRA - VOCAB), (0, 0)))]
    unnamed x1 -> x4, local copies, waits for them, and re-layouts: 2.46 us -> 3.04 us
where the time goes in v2:
time: 101 us
  Pallas kernels  97.3 us (96%)
  local copies, waits for them, and re-layouts  3.04 us (3%)
    pallas_call x1, Pallas kernels, on_device(): pl.pallas_call(kernel, out_shape=(jax.ShapeDtypeStruct((ROWS, D), BF16),...  97.3 us
    unnamed x4, local copies, waits for them, and re-layouts  3.04 us

profile of v2, /device:TPU:41, one launch (start us, length us, event | category | flops | bytes accessed | tf_op | source)
XLA Modules:
  0.0 101.0 jit_solution(2897265969894793229)
XLA Ops:
  0.6 97.3 %shard_map.104 = (bf16[512,1280]{1,0:T(8,128)(2,1)}, f32[4,1,128]{2,1,0:T(1,128)}) custom-call(bf16[512,1280]{1,0:T(8,128)(2,1)} %x_hbm.1, s32[4,1,128]{2,1,0:T(1,128)} %bitcast.2, bf16[5,1280]{1,0:T(8,128)(2,1)} %decoder.1, bf16[1280,640]{1,0:T(8,128)(2,1)} %sq_i_hbm.1, bf16[3,640,640]{2,1,0:T(8,128)(2,1)} %taps_i_hbm.1, bf16[640,1280]{1,0:T(8,128)(2,1)} %ex_i_hbm.1, ...), custom_call_target="tpu_custom_call" | custom-call | tf_op jit(solution)/shard_map/pallas_call | solution.py:403
  98.0 0.0 copy-start
  98.0 2.5 %copy.13 = bf16[512,1280]{1,0:T(8,128)(2,1)} copy(bf16[512,1280]{1,0:T(8,128)(2,1)} %get-tuple-element.8) | data formatting | bytes 2621440
  100.4 0.0 copy-done
  100.4 0.6 copy.14
Async XLA Ops:
  98.0 2.5 %copy-start = (f32[4,1,128]{2,1,0:T(1,128)S(1)}, f32[4,1,128]{2,1,0:T(1,128)}, u32[]{:S(2)}) copy-start(f32[4,1,128]{2,1,0:T(1,128)} %get-tuple-element.5) | copy-start | bytes 6148

commit v3 on v2

--- a/solution.py
+++ b/solution.py
@@ -191,6 +191,8 @@
         tiles(first)
 
     def converse(k):
+        rows = at(k, 0, CH)
+        narrow[...] = dot(mid[rows, :], taps_i[1])
         for copy in mid_halos(k):
             copy.wait_recv()
 
@@ -199,10 +201,7 @@
             for copy in mid_halos(k + 1):
                 copy.start()
 
-        rows = at(k, 0, CH)
-        narrow[...] = (
-            dot(mid_behind[rows, :], taps_i[0]) + dot(mid[rows, :], taps_i[1]) + dot(mid_ahead[rows, :], taps_i[2])
-        )
+        narrow[...] += dot(mid_behind[rows, :], taps_i[0]) + dot(mid_ahead[rows, :], taps_i[2])
 
         def first(r):
             n, factor = normed(narrow[pl.ds(r, TILE), :])
@@ -327,14 +326,11 @@
 
     def leave(k):
         loss_out[k] = dot_t(jnp.ones((8, EXTRA), BF16), g[at(k, 0, CH), D:])[0:1]
+        rows = at(k, 0, CH)
+        narrow[...] = dot_t(dconv[rows, :], taps_i[1])
         for copy in dconv_halos(k):
             copy.wait_recv()
-        rows = at(k, 0, CH)
-        narrow[...] = (
-            dot_t(dconv_ahead[rows, :], taps_i[0])
-            + dot_t(dconv[rows, :], taps_i[1])
-            + dot_t(dconv_behind[rows, :], taps_i[2])
-        )
+        narrow[...] += dot_t(dconv_ahead[rows, :], taps_i[0]) + dot_t(dconv_behind[rows, :], taps_i[2])
 
         def first(r):
             upward = sl_mid[at(k, r), :] * narrow[pl.ds(r, TILE), :]
@@ -403,8 +399,8 @@
     out, loss = pl.pallas_call(
         kernel,
         out_shape=(
-            jax.ShapeDtypeStruct((ROWS, D), BF16),
-            jax.ShapeDtypeStruct((CHUNKS, 1, CH), F32),
+            pltpu.VMEM((ROWS, D), BF16),
+            pltpu.VMEM((CHUNKS, 1, CH), F32),
         ),
         in_specs=[anywhere, vmem, vmem] + [anywhere] * 6,
         out_specs=(vmem, vmem),

time: 101 us -> 98 us (0.970)
  Pallas kernels: 97.3 us -> 95.6 us
  local copies, waits for them, and re-layouts: 3.04 us -> 1.64 us
    pallas_call x1, Pallas kernels: 97.3 us -> 95.6 us  [on_device(): pl.pallas_call(kernel, out_shape=(pltpu.VMEM((ROWS, D), BF16), pltpu.VMEM...]
    unnamed x4 -> x2, local copies, waits for them, and re-layouts: 3.04 us -> 1.64 us
where the time goes in v3:
time: 98 us; the launch traced here: 97.9 us
  Pallas kernels  95.6 us (98%)
  local copies, waits for them, and re-layouts  1.64 us (2%)
    pallas_call x1, Pallas kernels, on_device(): pl.pallas_call(kernel, out_shape=(pltpu.VMEM((ROWS, D), BF16), pltpu.VMEM...  95.6 us

profile of v3, /device:TPU:41, one launch (start us, length us, event | category | flops | bytes accessed | tf_op | source)
XLA Modules:
  0.0 97.9 jit_solution(2153128200319075124)
XLA Ops:
  0.6 95.6 %shard_map.104 = (bf16[512,1280]{1,0:T(8,128)(2,1)S(1)}, f32[4,1,128]{2,1,0:T(1,128)S(1)}) custom-call(bf16[512,1280]{1,0:T(8,128)(2,1)} %x_hbm.1, s32[4,1,128]{2,1,0:T(1,128)} %bitcast.3, bf16[5,1280]{1,0:T(8,128)(2,1)} %decoder.1, bf16[1280,640]{1,0:T(8,128)(2,1)} %sq_i_hbm.1, bf16[3,640,640]{2,1,0:T(8,128)(2,1)} %taps_i_hbm.1, ...), custom_call_target="tpu_custom_call" | custom-call | tf_op jit(solution)/shard_map/pallas_call | solution.py:399
  96.2 1.1 %copy.13 = bf16[512,1280]{1,0:T(8,128)(2,1)} copy(bf16[512,1280]{1,0:T(8,128)(2,1)S(1)} %get-tuple-element.6) | data formatting | bytes 2621440
  97.3 0.6 copy.14

commit v4 on v3

--- a/solution.py
+++ b/solution.py
@@ -16,7 +16,7 @@
 CH = ROWS // CHUNKS
 QUARTER = CH // 4
 EXTRA = 128
-WIDE = D + EXTRA
+AHEAD = 4
 TILE = 16
 
 
@@ -67,18 +67,22 @@
     x, sq_i, taps_i, ex_i, sq_o, taps_o, ex_o,
     n_in, f_in, n_mid, f_mid, n_conv, f_conv, sl_in, sl_mid,
     mid, mid_behind, mid_ahead, dconv, dconv_behind, dconv_ahead,
-    xo_send, xo, g_send, g,
+    xo, g, outs_send, hot_send, hot, loss_send, loss_back,
     ent, wide, narrow,
     o_n_in, o_f_in, o_n_mid, o_f_mid, o_n_conv, o_f_conv, o_grad, o_mid, o_dconv, dec,
-    w_sem, x_sem, own_sem, halo_send, halo_recv, turn_send, turn_recv,
+    w_sem, own_sem, halo_send, halo_recv, turn_send, turn_recv,
 ):
     c, f = lax.axis_index("coarse"), lax.axis_index("fine")
     shard = c * 16 + f
     mine = c // 4
 
+    along = lax.rem(c, 4) * 16 + f
+
     def inner_partner(way):
-        other = lax.rem(shard + (2 if way == 0 else 254), 256)
-        return (other // 16, lax.rem(other, 16))
+        other = lax.rem(along + (2 if way == 0 else 62), 64)
+        return (mine * 4 + other // 16, lax.rem(other, 16))
+
+    shifts = ((along + 2) // 64, 3 * (1 - (along + 62) // 64))
 
     def outer_partner(i):
         return (lax.rem(c + 4 * i, 16), f)
@@ -86,10 +90,6 @@
     barrier = pltpu.get_barrier_semaphore()
     for partner in (inner_partner(0), inner_partner(1), outer_partner(1), outer_partner(2), outer_partner(3)):
         pl.semaphore_signal(barrier, inc=1, device_id=partner, device_id_type=MESH)
-
-    def x_copy(k):
-        rows = pl.ds(pl.multiple_of(k * CH, CH), CH)
-        return pltpu.make_async_copy(x_hbm.at[rows], x.at[rows], x_sem.at[k])
 
     weights = [
         pltpu.make_async_copy(src, dst, w_sem.at[i])
@@ -100,23 +100,30 @@
             )
         )
     ]
-    x_copy(0).start()
-    weights[0].start()
-    for k in range(1, CHUNKS):
-        x_copy(k).start()
-    for weight in weights[1:]:
+    for weight in weights:
         weight.start()
 
-    def halo(stage, way, k, source, target):
-        rows = pl.ds(pl.multiple_of(k * CH, CH), CH)
+    def copy_rows(stage, way, k, source, source_rows, target, target_rows):
         return pltpu.make_async_remote_copy(
-            src_ref=source.at[rows],
-            dst_ref=target.at[rows],
+            src_ref=source.at[source_rows],
+            dst_ref=target.at[target_rows],
             send_sem=halo_send.at[stage, way, k],
             recv_sem=halo_recv.at[stage, way, k],
             device_id=inner_partner(way),
             device_id_type=MESH,
         )
+
+    def halo(stage, way, k, source, target):
+        rows = pl.ds(pl.multiple_of(k * CH, CH), CH)
+        return copy_rows(stage, way, k, source, rows, target, rows)
+
+    def send_halos(stage, k, source, targets_pair):
+        for way in (0, 1):
+            for block in range(4):
+                there = lax.rem(block + shifts[way], 4)
+                copy_rows(
+                    stage, way, k, source, quarter(k, block), targets_pair[way], quarter(k, there)
+                ).start()
 
     def mid_halos(k):
         return halo(0, 0, k, mid, mid_behind), halo(0, 1, k, mid, mid_ahead)
@@ -139,7 +146,7 @@
         )
 
     def turns(stage, k):
-        source, target = ((xo_send, xo), (g_send, g))[stage]
+        source, target = ((x_hbm, x), (outs_send, outs), (hot_send, hot), (loss_send, loss_back))[stage]
         return [turn(stage, i, k, source, target) for i in (1, 2, 3)] + [
             pltpu.make_async_copy(source.at[quarter(k, mine)], target.at[quarter(k, mine)], own_sem.at[stage, k])
         ]
@@ -154,7 +161,7 @@
         return pl.ds(pl.multiple_of(k * CH + r, TILE), rows)
 
     def enter(k):
-        x_copy(k).wait()
+        await_turns(0, k)
 
         def first(r):
             n, factor = normed(x[at(k, r), :].astype(F32))
@@ -173,16 +180,17 @@
 
         tiles(second)
 
-        @pl.when(k < 1)
+        @pl.when(k < AHEAD)
         def _():
-            for copy in mid_halos(k):
-                copy.start()
+            send_halos(0, k, mid, (mid_behind, mid_ahead))
 
     def prepare(k):
         classes = lax.broadcasted_iota(jnp.int32, (EXTRA, CH), 0)
         columns = (classes == targets[k]).astype(F32).astype(BF16)
         eye = (classes == lax.broadcasted_iota(jnp.int32, (EXTRA, CH), 1)).astype(F32).astype(BF16)
-        xo_send[at(k, 0, CH), D:] = dot_t(eye, columns).astype(BF16)
+        hot_send[at(k, 0, CH), :] = dot_t(eye, columns).astype(BF16)
+        for copy in turns(2, k):
+            copy.start()
 
         def first(r):
             sl_in[at(k, r), :] = slope(n_in[at(k, r), :])
@@ -196,28 +204,25 @@
         for copy in mid_halos(k):
             copy.wait_recv()
 
-        @pl.when(k + 1 < CHUNKS)
+        @pl.when(k + AHEAD < CHUNKS)
         def _():
-            for copy in mid_halos(k + 1):
-                copy.start()
+            send_halos(0, k + AHEAD, mid, (mid_behind, mid_ahead))
 
         narrow[...] += dot(mid_behind[rows, :], taps_i[0]) + dot(mid_ahead[rows, :], taps_i[2])
 
         def first(r):
             n, factor = normed(narrow[pl.ds(r, TILE), :])
-            n_conv[at(k, r), :] = n
-            f_conv[at(k, r), :] = lanes(factor)
+            n_conv[pl.ds(r, TILE), :] = n
+            f_conv[pl.ds(r, TILE), :] = lanes(factor)
             ent[pl.ds(r, TILE), :BOT] = gelu(n).astype(BF16)
 
         tiles(first)
         wide[...] = dot(ent[:, :BOT], ex_i[...])
 
         def second(r):
-            xo_send[at(k, r), :D] = (x[at(k, r), :].astype(F32) + wide[pl.ds(r, TILE), :]).astype(BF16)
+            xo[pl.ds(r, TILE), :] = (x[at(k, r), :].astype(F32) + wide[pl.ds(r, TILE), :]).astype(BF16)
 
         tiles(second)
-        for copy in turns(0, k):
-            copy.start()
 
     def around(padded):
         padded[pl.ds(0, QUARTER), :] = padded[pl.ds(CH, QUARTER), :]
@@ -225,10 +230,8 @@
         return padded[pl.ds(0, CH), :], padded[pl.ds(QUARTER, CH), :], padded[pl.ds(2 * QUARTER, CH), :]
 
     def outer(k):
-        await_turns(0, k)
-
-        def first(r):
-            n, factor = normed(xo[at(k, r), :D].astype(F32))
+        def first(r):
+            n, factor = normed(xo[pl.ds(r, TILE), :].astype(F32))
             o_n_in[pl.ds(r, TILE), :] = n
             o_f_in[pl.ds(r, TILE), :] = lanes(factor)
             ent[pl.ds(r, TILE), :] = gelu(n).astype(BF16)
@@ -256,7 +259,7 @@
         wide[...] = dot(ent[:, :BOT], ex_o[...])
 
         def fourth(r):
-            final = (xo[at(k, r), :D].astype(F32) + wide[pl.ds(r, TILE), :]).astype(BF16)
+            final = (xo[pl.ds(r, TILE), :].astype(F32) + wide[pl.ds(r, TILE), :]).astype(BF16)
             n, factor = normed(final.astype(F32))
             o_grad[pl.ds(r, TILE), :] = n
             narrow[pl.ds(r, TILE), :128] = lanes(factor)
@@ -264,15 +267,18 @@
 
         tiles(fourth)
         logits = dot_t(ent[...], dec[...])
+        await_turns(2, k)
         lane = lax.broadcasted_iota(jnp.int32, (CH, EXTRA), 1)
-        onehot = xo[at(k, 0, CH), D:].astype(F32)
+        onehot = hot[at(k, 0, CH), :].astype(F32)
         exponent = jnp.where(lane < VOCAB, jnp.exp(logits), 0.0)
         totals = jnp.sum(exponent, axis=-1, keepdims=True)
         token_loss = jnp.log(totals) - jnp.sum(logits * onehot, axis=-1, keepdims=True)
         high = token_loss.astype(BF16).astype(F32)
-        g_send[at(k, 0, CH), D:] = jnp.where(
+        loss_send[at(k, 0, CH), :] = jnp.where(
             lane == 0, high, jnp.where(lane == 1, token_loss - high, 0.0)
         ).astype(BF16)
+        for copy in turns(3, k):
+            copy.start()
         dlogits = (32.0 * (exponent / totals - onehot)).astype(BF16)
         wide[...] = dot(dlogits, dec[...])
 
@@ -305,27 +311,24 @@
             n = o_n_in[pl.ds(r, TILE), :]
             upward = slope(n) * wide[pl.ds(r, TILE), :]
             back = norm_back(n, o_f_in[pl.ds(r, TILE), 0:1], upward)
-            g_send[at(k, r), :D] = (o_grad[pl.ds(r, TILE), :] + back).astype(BF16)
+            total = o_grad[pl.ds(r, TILE), :] + back
+            g[at(k, r), :] = total
+            ent[pl.ds(r, TILE), :] = total.astype(BF16)
 
         tiles(eighth)
-        for copy in turns(1, k):
-            copy.start()
 
     def turn_back(k):
-        await_turns(1, k)
-        narrow[...] = dot_t(g[at(k, 0, CH), :D], ex_i[...])
-
-        def first(r):
-            n = n_conv[at(k, r), :]
+        narrow[...] = dot_t(ent[...], ex_i[...])
+
+        def first(r):
+            n = n_conv[pl.ds(r, TILE), :]
             upward = slope(n) * narrow[pl.ds(r, TILE), :]
-            dconv[at(k, r), :] = norm_back(n, f_conv[at(k, r), 0:1], upward).astype(BF16)
-
-        tiles(first)
-        for copy in dconv_halos(k):
-            copy.start()
+            dconv[at(k, r), :] = norm_back(n, f_conv[pl.ds(r, TILE), 0:1], upward).astype(BF16)
+
+        tiles(first)
+        send_halos(1, k, dconv, (dconv_behind, dconv_ahead))
 
     def leave(k):
-        loss_out[k] = dot_t(jnp.ones((8, EXTRA), BF16), g[at(k, 0, CH), D:])[0:1]
         rows = at(k, 0, CH)
         narrow[...] = dot_t(dconv[rows, :], taps_i[1])
         for copy in dconv_halos(k):
@@ -342,9 +345,11 @@
         def second(r):
             upward = sl_in[at(k, r), :] * wide[pl.ds(r, TILE), :]
             back = norm_back(n_in[at(k, r), :], f_in[at(k, r), 0:1], upward)
-            outs[at(k, r), :] = (g[at(k, r), :D].astype(F32) + back).astype(BF16)
+            outs_send[at(k, r), :] = (g[at(k, r), :] + back).astype(BF16)
 
         tiles(second)
+        for copy in turns(1, k):
+            copy.start()
 
     def loop(count, body):
         def step(k, carry):
@@ -356,34 +361,33 @@
     dec[...] = jnp.zeros_like(dec)
     dec[pl.ds(0, VOCAB), :] = decoder[...]
     pl.semaphore_wait(barrier, 5)
+
+    def fetch(k):
+        for copy in turns(0, k):
+            copy.start()
+
+    loop(CHUNKS, fetch)
     weights[0].wait()
     loop(CHUNKS, enter)
     loop(CHUNKS, prepare)
     for weight in weights[1:]:
         weight.wait()
 
-    def middle(step):
-        s = step - 1
-
-        @pl.when(s + 1 < CHUNKS)
-        def _():
-            converse(s + 1)
-
-        @pl.when(jnp.logical_and(s >= 0, s < CHUNKS))
-        def _():
-            outer(s)
-
-        @pl.when(s >= 1)
-        def _():
-            turn_back(s - 1)
-
-    loop(CHUNKS + 2, middle)
+    def middle(k):
+        converse(k)
+        outer(k)
+        turn_back(k)
+
+    loop(CHUNKS, middle)
     loop(CHUNKS, leave)
 
     def finish(k):
         for copy in mid_halos(k) + dconv_halos(k):
             copy.wait_send()
-        for stage in (0, 1):
+        await_turns(3, k)
+        loss_out[k] = dot_t(jnp.ones((8, EXTRA), BF16), loss_back[at(k, 0, CH), :])[0:1]
+        await_turns(1, k)
+        for stage in range(4):
             for copy in turns(stage, k)[:3]:
                 copy.wait_send()
 
@@ -414,13 +418,14 @@
             v((ROWS, D), F32), v((ROWS, BOT), F32),
             v((ROWS, BOT), BF16), v((ROWS, BOT), BF16), v((ROWS, BOT), BF16),
             v((ROWS, BOT), BF16), v((ROWS, BOT), BF16), v((ROWS, BOT), BF16),
-            v((ROWS, WIDE), BF16), v((ROWS, WIDE), BF16), v((ROWS, WIDE), BF16), v((ROWS, WIDE), BF16),
+            v((CH, D), BF16), v((ROWS, D), F32), v((ROWS, D), BF16),
+            v((ROWS, EXTRA), BF16), v((ROWS, EXTRA), BF16), v((ROWS, EXTRA), BF16), v((ROWS, EXTRA), BF16),
             v((CH, D), BF16), v((CH, D), F32), v((CH, BOT), F32),
             v((CH, D), F32), v((CH, 128), F32), v((CH, BOT), F32), v((CH, 128), F32),
             v((CH, BOT), F32), v((CH, 128), F32), v((CH, D), F32),
             v((CH + 2 * QUARTER, BOT), BF16), v((CH + 2 * QUARTER, BOT), BF16), v((EXTRA, D), BF16),
-            dma((6,)), dma((CHUNKS,)), dma((2, CHUNKS)),
-            dma((2, 2, CHUNKS)), dma((2, 2, CHUNKS)), dma((2, 4, CHUNKS)), dma((2, 4, CHUNKS)),
+            dma((6,)), dma((4, CHUNKS)),
+            dma((2, 2, CHUNKS)), dma((2, 2, CHUNKS)), dma((4, 4, CHUNKS)), dma((4, 4, CHUNKS)),
         ],
         compiler_params=pltpu.CompilerParams(
             collective_id=0, has_side_effects=True, vmem_limit_bytes=62 * 1024 * 1024

time: 98 us -> 95.2 us (0.971)
  the two profiles are of different devices: /device:TPU:41 before, /device:TPU:1 now
where the time goes in v4:
time: 95.2 us; the launch traced here: 95 us
  Pallas kernels  92.8 us (97%)
  local copies, waits for them, and re-layouts  1.64 us (2%)
    pallas_call x1, Pallas kernels, on_device(): pl.pallas_call(kernel, out_shape=(pltpu.VMEM((ROWS, D), BF16), pltpu.VMEM...  92.8 us

profile of v4, /device:TPU:1, one launch (start us, length us, event | category | flops | bytes accessed | tf_op | source)
XLA Modules:
  0.0 95.0 jit_solution(589650876311784215)
XLA Ops:
  0.6 92.8 %shard_map.104 = (bf16[512,1280]{1,0:T(8,128)(2,1)S(1)}, f32[4,1,128]{2,1,0:T(1,128)S(1)}) custom-call(bf16[512,1280]{1,0:T(8,128)(2,1)} %x_hbm.1, s32[4,1,128]{2,1,0:T(1,128)} %bitcast.3, bf16[5,1280]{1,0:T(8,128)(2,1)} %decoder.1, bf16[1280,640]{1,0:T(8,128)(2,1)} %sq_i_hbm.1, bf16[3,640,640]{2,1,0:T(8,128)(2,1)} %taps_i_hbm.1, ...), custom_call_target="tpu_custom_call" | custom-call | tf_op jit(solution)/shard_map/pallas_call | solution.py:403
  93.4 1.1 %copy.13 = bf16[512,1280]{1,0:T(8,128)(2,1)} copy(bf16[512,1280]{1,0:T(8,128)(2,1)S(1)} %get-tuple-element.6) | data formatting | bytes 2621440
  94.5 0.6 copy.14

commit v5 on v4

--- a/solution.py
+++ b/solution.py
@@ -16,7 +16,7 @@
 CH = ROWS // CHUNKS
 QUARTER = CH // 4
 EXTRA = 128
-AHEAD = 4
+AHEAD = 3
 TILE = 16
 
 

time: 95.2 us -> 94.3 us (level)
  the two profiles are of different devices: /device:TPU:1 before, /device:TPU:41 now
where the time goes in v5:
time: 94.3 us; the launch traced here: 93.2 us
  Pallas kernels  90.9 us (96%)
  local copies, waits for them, and re-layouts  1.64 us (2%)
    pallas_call x1, Pallas kernels, on_device(): pl.pallas_call(kernel, out_shape=(pltpu.VMEM((ROWS, D), BF16), pltpu.VMEM...  90.9 us

profile of v5, /device:TPU:41, one launch (start us, length us, event | category | flops | bytes accessed | tf_op | source)
XLA Modules:
  0.0 93.2 jit_solution(11957575827826949780)
XLA Ops:
  0.6 90.9 %shard_map.104 = (bf16[512,1280]{1,0:T(8,128)(2,1)S(1)}, f32[4,1,128]{2,1,0:T(1,128)S(1)}) custom-call(bf16[512,1280]{1,0:T(8,128)(2,1)} %x_hbm.1, s32[4,1,128]{2,1,0:T(1,128)} %bitcast.3, bf16[5,1280]{1,0:T(8,128)(2,1)} %decoder.1, bf16[1280,640]{1,0:T(8,128)(2,1)} %sq_i_hbm.1, bf16[3,640,640]{2,1,0:T(8,128)(2,1)} %taps_i_hbm.1, ...), custom_call_target="tpu_custom_call" | custom-call | tf_op jit(solution)/shard_map/pallas_call | solution.py:403
  91.6 1.1 %copy.13 = bf16[512,1280]{1,0:T(8,128)(2,1)} copy(bf16[512,1280]{1,0:T(8,128)(2,1)S(1)} %get-tuple-element.6) | data formatting | bytes 2621440
  92.6 0.6 copy.14
